TPU v7x, 512 devices: a whole 4x8x8 slice. The times are simulated.
512 devices in a mesh: dom: 128 (over z, y, core), sub: 4 (over x).
Axes of the slice: x: 4, y: 8, z: 8, core: 2. Of those that a mesh axis runs over, the one named last changes fastest.
Arguments:
- fine_nodes: float32 [524288, 128], P(('dom', 'sub')), may hold values from -6 to 6
- fine_edges: float32 [6, 524288, 128], P(None, ('dom', 'sub')), may hold values from -6 to 6
- fine_nbr: int32 [6, 524288], P(None, ('dom', 'sub')), may hold values from 0 to 1599, as said below
- sub_send: int32 [512, 4, 96], P(('dom', 'sub')), may hold values from 0 to 1023
- dom_send: int32 [512, 2, 96], P(('dom', 'sub')), may hold values from 0 to 1023
- pool_owner: int32 [524288, 1], P(('dom', 'sub')), may hold values from 0 to 127, as said below
- pool_slot: int32 [524288], P(('dom', 'sub')), may hold values from 0 to 255
- coarse_nbr: int32 [6, 131072], P(None, ('dom', 'sub')), may hold values from 0 to 383, as said below
- coarse_send: int32 [512, 2, 64], P(('dom', 'sub')), may hold values from 0 to 255
- fine_edge_in: float32 [384, 128], replicated, may hold values from -0.3125 to 0.3125
- fine_edge_out: float32 [128, 128], replicated, may hold values from -0.5 to 0.5
- fine_node_in: float32 [256, 128], replicated, may hold values from -0.375 to 0.375
- fine_node_out: float32 [128, 128], replicated, may hold values from -0.5 to 0.5
- coarse_edge_in: float32 [256, 128], replicated, may hold values from -0.375 to 0.375
- coarse_edge_out: float32 [128, 128], replicated, may hold values from -0.5 to 0.5
- coarse_node_in: float32 [256, 128], replicated, may hold values from -0.375 to 0.375
- coarse_node_out: float32 [128, 128], replicated, may hold values from -0.5 to 0.5
Outputs:
- fine_out: float32 [524288, 128], P(('dom', 'sub'))
Inputs may be any that keep to these rules, and one draw needn't show every extreme that they name: `fine_nbr`: indexes the device's 1024 own rows, then 4 blocks of 96 rows from the siblings along sub in order, then 96 rows from the previous and 96 from the next device along dom. `sub_send`: local rows of the sending device. `dom_send`: slot 0 goes to the next device along dom, slot 1 to the previous; local rows of the sender. `pool_owner`: the owner is the device with this dom index and the same sub index; it is the row's own dom index or one next to it; among the rows of one device exactly 128 name the next dom index and exactly 128 the previous one where these exist, the others their own. `coarse_nbr`: indexes the device's 256 own coarse rows, then 64 rows from the previous and 64 from the next device along dom. `coarse_send`: slot 0 goes to the next device along dom, slot 1 to the previous; local coarse rows of the sender.
All inputs are finite; a program needn't handle non-finite values.
Results may differ from a plain program's by a relative error of at most 0.0003.
Values sent between devices are 32-bit elements; how exact they have to be, the bound alone decides.
No kernel may reach another device: no remote copies, remote signals or barrier semaphores. Data moves between devices by JAX's collectives and lax.ppermute only.
A program may use at most 64 MiB of HBM per device.

v0:
```python
import jax
import jax.numpy as jnp
from jax import lax
from jax.sharding import PartitionSpec as P

highest = lax.Precision.HIGHEST


def shifted_2(block, axis, distance):
    devices = range(lax.axis_size(axis))
    route = [(i - distance, i) for i in devices if i - distance in devices]
    return lax.ppermute(block, axis, route)


def layer_norm(values):
    centre = jnp.mean(values, axis=-1, keepdims=True)
    shifted = values - centre
    spread = jnp.mean(shifted * shifted, axis=-1, keepdims=True)
    return shifted * lax.rsqrt(spread + 1e-05)


def message_layer(
    latent_own, extended, neighbours, edge_latent, edge_in, edge_out, node_in, node_out
):
    features = latent_own.shape[1]
    degree, count_rows = neighbours.shape
    from_own = jnp.dot(latent_own, edge_in[:features], precision=highest)
    from_table = jnp.dot(extended, edge_in[features : 2 * features], precision=highest)
    pre_act = from_own[None, :, :] + from_table[neighbours.reshape(-1)].reshape(
        degree, count_rows, features
    )
    if edge_latent is not None:
        from_edges = jnp.dot(
            edge_latent.reshape(-1, features), edge_in[2 * features :], precision=highest
        )
        pre_act = pre_act + from_edges.reshape(degree, count_rows, features)
    hidden = jax.nn.relu(pre_act).reshape(-1, features)
    message = layer_norm(jnp.dot(hidden, edge_out, precision=highest)).reshape(
        degree, count_rows, features
    )
    if edge_latent is not None:
        message = edge_latent + message
    summed = jnp.sum(message, axis=0)
    node_pre = jnp.dot(latent_own, node_in[:features], precision=highest) + jnp.dot(
        summed, node_in[features:], precision=highest
    )
    return latent_own + layer_norm(jnp.dot(jax.nn.relu(node_pre), node_out, precision=highest))


def local(
    fine_nodes,
    fine_edges,
    fine_nbr,
    sub_send,
    dom_send,
    pool_owner,
    pool_slot,
    coarse_nbr,
    coarse_send,
    fine_edge_in,
    fine_edge_out,
    fine_node_in,
    fine_node_out,
    coarse_edge_in,
    coarse_edge_out,
    coarse_node_in,
    coarse_node_out,
):
    features = fine_nodes.shape[1]
    node_rows = fine_nodes.shape[0]
    packed = fine_nodes[sub_send[0]]
    everyone = lax.all_gather(packed[None], "sub", axis=0, tiled=True)
    sibling_rows = lax.dynamic_index_in_dim(everyone, lax.axis_index("sub"), 1, keepdims=False)
    dom_lists = dom_send[0]
    beside = []
    for offset, column in ((1, 0), (-1, 1)):
        beside.append(shifted_2(fine_nodes[dom_lists[column]], "dom", offset))
    fine_table = jnp.concatenate([fine_nodes, sibling_rows.reshape(-1, features)] + beside, axis=0)
    fine_mid = message_layer(
        fine_nodes,
        fine_table,
        fine_nbr,
        fine_edges,
        fine_edge_in,
        fine_edge_out,
        fine_node_in,
        fine_node_out,
    )
    capacity = node_rows // 8
    owner_step = pool_owner[:, 0] - lax.axis_index("dom")
    go_next = owner_step == 1
    go_prev = owner_step == -1
    rank_next = jnp.cumsum(go_next.astype(jnp.int32)) - 1
    rank_prev = jnp.cumsum(go_prev.astype(jnp.int32)) - 1
    shifted_slots = pool_slot + 1
    received_rows = []
    received_slots = []
    for offset, chosen, rank in ((1, go_next, rank_next), (-1, go_prev, rank_prev)):
        destination = jnp.where(chosen, rank, capacity)
        out_rows = (
            jnp.zeros((capacity, features), jnp.float32).at[destination].set(fine_mid, mode="drop")
        )
        out_slots = (
            jnp.zeros((capacity,), jnp.int32).at[destination].set(shifted_slots, mode="drop")
        )
        got_rows, got_slots = shifted_2((out_rows, out_slots), "dom", offset)
        received_rows.append(got_rows)
        received_slots.append(got_slots - 1)
    own_slots = jnp.where(owner_step == 0, pool_slot, -1)
    all_slots = jnp.concatenate([own_slots] + received_slots, axis=0)
    all_rows = jnp.concatenate([fine_mid] + received_rows, axis=0)
    coarse_count = coarse_nbr.shape[1]
    member = (all_slots[None, :] == jnp.arange(coarse_count, dtype=jnp.int32)[:, None]).astype(
        jnp.float32
    )
    sums = jnp.dot(member, all_rows, precision=highest)
    counts = jnp.sum(member, axis=1)
    pooled = sums / jnp.maximum(counts, 1.0)[:, None]
    coarse_lists = coarse_send[0]
    coarse_beside = []
    for offset, column in ((1, 0), (-1, 1)):
        coarse_beside.append(shifted_2(pooled[coarse_lists[column]], "dom", offset))
    coarse_table = jnp.concatenate([pooled] + coarse_beside, axis=0)
    refined = message_layer(
        pooled,
        coarse_table,
        coarse_nbr,
        None,
        coarse_edge_in,
        coarse_edge_out,
        coarse_node_in,
        coarse_node_out,
    )
    answers = lax.dot_general(member, refined, (((0,), (0,)), ((), ())), precision=highest)
    own_answers = answers[:node_rows]
    returned = []
    for offset, start in ((-1, node_rows), (1, node_rows + capacity)):
        returned.append(shifted_2(answers[start : start + capacity], "dom", offset))
    from_next = returned[0][jnp.clip(rank_next, 0, capacity - 1)]
    from_prev = returned[1][jnp.clip(rank_prev, 0, capacity - 1)]
    chosen_answers = jnp.where(
        go_next[:, None], from_next, jnp.where(go_prev[:, None], from_prev, own_answers)
    )
    return fine_mid + chosen_answers


def solution(mesh):
    in_specs = (
        P(("dom", "sub"), None),
        P(None, ("dom", "sub"), None),
        P(None, ("dom", "sub")),
        P(("dom", "sub"), None, None),
        P(("dom", "sub"), None, None),
        P(("dom", "sub"), None),
        P(("dom", "sub")),
        P(None, ("dom", "sub")),
        P(("dom", "sub"), None, None),
        P(),
        P(),
        P(),
        P(),
        P(),
        P(),
        P(),
        P(),
    )
    out_specs = P(("dom", "sub"), None)
    return jax.shard_map(local, mesh=mesh, in_specs=in_specs, out_specs=out_specs, check_vma=False)
```

profile of v0, /device:TPU:255, one launch (start us, length us, event | category | flops | bytes accessed | tf_op | source)
XLA Modules:
  0.0 151.2 jit_solution(4779850287646350684)
XLA Ops:
  0.0 0.8 fusion.56
  0.8 2.3 %gather_fusion.1 = f32[96,128]{1,0:T(8,128)} fusion(f32[1024,128]{1,0:T(8,128)} %param.17, s32[1024]{0:T(1024)S(1)} %pad_clamp_fusion.4), kind=kCustom, calls=%fused_computation.1 | custom fusion | bytes 98688 | tf_op jit(solution)/shard_map/gather | solution.py:77
  3.1 5.0 %collective-permute-start = (f32[96,128]{1,0:T(8,128)}, f32[96,128]{1,0:T(8,128)}, u32[]{:S(2)}, u32[]{:S(2)}) collective-permute-start(f32[96,128]{1,0:T(8,128)} %gather_fusion.1), channel_id=1, source_target_pairs={{0,4},{4,8},{8,12},{12,16},{16,20},{20,24},{24,28},{28,32},{32,36}... | collective-permute-start | bytes 147464 | tf_op jit(solution)/shard_map/ppermute | solution.py:12
  8.0 2.3 %gather_fusion.2 = f32[96,128]{1,0:T(8,128)} fusion(f32[1024,128]{1,0:T(8,128)} %param.17, s32[1024]{0:T(1024)S(1)} %pad_clamp_fusion.3), kind=kCustom, calls=%fused_computation.2 | custom fusion | bytes 98688 | tf_op jit(solution)/shard_map/gather | solution.py:77
  10.3 1.9 %collective-permute-start.1 = (f32[96,128]{1,0:T(8,128)}, f32[96,128]{1,0:T(8,128)}, u32[]{:S(2)}, u32[]{:S(2)}) collective-permute-start(f32[96,128]{1,0:T(8,128)} %gather_fusion.2), channel_id=1, source_target_pairs={{4,0},{8,4},{12,8},{16,12},{20,16},{24,20},{28,24},{32,28},{36,32}... | collective-permute-start | bytes 147464 | tf_op jit(solution)/shard_map/ppermute | solution.py:12
  12.2 1.3 fusion.53
  13.5 0.3 reduce-window.16
  14.1 0.3 reduce-window.24
  14.7 0.7 compare_select_fusion.2
  15.4 0.7 broadcast_select_fusion
  16.1 4.8 %scatter_custom_fusion.1 = s32[128]{0:T(128)} fusion(s32[1024]{0:T(1024)S(1)} %bitcast.84, s32[1024]{0:T(1024)S(1)} %get-tuple-element.15, s32[]{:T(128)} %constant.24.clone.1), kind=kCustom, calls=%fused_computation.130 | custom fusion | bytes 516 | tf_op jit(solution)/shard_map/scatter | solution.py:104
  20.9 1.9 %collective-permute-start.3 = (s32[128]{0:T(128)}, s32[128]{0:T(128)}, u32[]{:S(2)}, u32[]{:S(2)}) collective-permute-start(s32[128]{0:T(128)} %scatter_custom_fusion.1), channel_id=1, source_target_pairs={{4,0},{8,4},{12,8},{16,12},{20,16},{24,20},{28,24},{32,28},{36,32}... | collective-permute-start | bytes 1544 | tf_op jit(solution)/shard_map/ppermute | solution.py:12
  22.9 4.8 %scatter_custom_fusion = s32[128]{0:T(128)} fusion(s32[1024]{0:T(1024)S(1)} %bitcast.86, s32[1024]{0:T(1024)S(1)} %get-tuple-element.15, s32[]{:T(128)} %constant.24.clone.1), kind=kCustom, calls=%fused_computation.132 | custom fusion | bytes 516 | tf_op jit(solution)/shard_map/scatter | solution.py:104
  27.6 7.0 %collective-permute-start.2 = (s32[128]{0:T(128)}, s32[128]{0:T(128)}, u32[]{:S(2)}, u32[]{:S(2)}) collective-permute-start(s32[128]{0:T(128)} %scatter_custom_fusion), channel_id=1, source_target_pairs={{0,4},{4,8},{8,12},{12,16},{16,20},{20,24},{24,28},{28,32},{32,36}... | collective-permute-start | bytes 1544 | tf_op jit(solution)/shard_map/ppermute | solution.py:12
  34.6 0.7 compare_select_fusion.6
  35.4 2.2 %gather_fusion = f32[384,128]{1,0:T(8,128)S(1)} fusion(f32[1024,128]{1,0:T(8,128)} %param.17, s32[1024]{0:T(1024)S(1)} %pad_clamp_fusion.5), kind=kCustom, calls=%fused_computation | custom fusion | bytes 394752 | tf_op jit(solution)/shard_map/gather | solution.py:71
  37.6 11.2 %all-gather = f32[16,96,128]{2,1,0:T(8,128)S(1)} all-gather(f32[4,96,128]{2,1,0:T(8,128)S(1)} %bitcast.72), channel_id=2, replica_groups=mesh['dom'=128,'sub'=4] {'sub'}, dimensions={0}, use_global_device_ids=true | all-gather | bytes 983040 | tf_op jit(solution)/shard_map/all_gather | solution.py:72
  48.8 0.6 fusion.43
  49.5 5.5 %fusion.30 = f32[6,1024,128]{2,1,0:T(8,128)} fusion(f32[6,1024,128]{2,1,0:T(8,128)} %param.18, f32[384,128]{1,0:T(8,128)S(1)} %copy-done.3), kind=kOutput, calls=%fused_computation.59 | convolution fusion | flops 1207959552 | bytes 6356992 | tf_op jit(solution)/shard_map/dot_general | solution.py:33
  55.0 0.6 fusion.45
  55.6 0.6 pad_clamp_fusion.2
  56.2 0.6 broadcast_clamp_fusion.1
  56.9 0.6 pad_clamp_fusion.1
  57.7 0.7 broadcast_add_fusion.1
  58.3 0.7 broadcast_add_fusion.2
  59.0 0.2 convert_reduce_fusion
  59.2 1.6 %fusion.5 = f32[1600,128]{1,0:T(8,128)S(1)} fusion(f32[96,128]{1,0:T(8,128)} %collective-permute-done.1, f32[96,128]{1,0:T(8,128)} %collective-permute-done, f32[384,128]{1,0:T(8,128)S(1)} %bitcast.71, f32[1024,128]{1,0:T(8,128)S(1)} %copy-done.1, f32[384,128]{1,0:T(8,128)S(1)} %copy-done.3), kind=kOutput, calls=%fused_computation.26 | convolution fusion | flops 315187200 | bytes 1703936 | tf_op jit(solution)/shard_map/dot_general | solution.py:28
  60.9 20.9 %gather_fusion.3 = f32[6144,128]{1,0:T(8,128)} fusion(f32[1600,128]{1,0:T(8,128)S(1)} %fusion.5, s32[6144]{0:T(1024)S(1)} %broadcast_clamp_fusion), kind=kCustom, calls=%fused_computation.3 | custom fusion | bytes 6316032 | tf_op jit(solution)/shard_map/gather | solution.py:29
  81.7 3.2 %add_maximum_fusion = f32[6,1024,128]{2,1,0:T(8,128)S(1)} fusion(f32[6,1024,128]{2,1,0:T(8,128)} %fusion.30, f32[6,1024,128]{2,1,0:T(8,128)} %bitcast.66, f32[1024,128]{1,0:T(8,128)S(1)} %fusion.43), kind=kLoop, calls=%fused_computation.15 | loop fusion | flops 2359296 | bytes 9961472 | tf_op jit(solution)/shard_map/jit(relu)/max | solution.py:37
  84.9 2.8 %fusion.68 = (f32[6144]{0:T(1024)S(1)}, f32[6144,128]{1,0:T(8,128)S(1)}) fusion(f32[6144,128]{1,0:T(8,128)S(1)} %bitcast.67, f32[128,128]{1,0:T(8,128)S(1)} %copy-done), kind=kOutput, calls=%fused_computation.139 | convolution fusion | flops 1208739840 | bytes 6381568 | tf_op jit(solution)/shard_map/dot_general | solution.py:38
  87.7 1.8 %multiply_reduce_fusion = f32[6144]{0:T(1024)S(1)} fusion(f32[6144,128]{1,0:T(8,128)S(1)} %get-tuple-element.23, f32[6144]{0:T(1024)S(1)} %broadcast_multiply_fusion), kind=kLoop, calls=%fused_computation.14 | loop fusion | flops 2353152 | bytes 3194880 | tf_op jit(solution)/shard_map/reduce_sum | solution.py:18
  89.6 3.3 %subtract_multiply_fusion = f32[6144,128]{1,0:T(8,128)S(1)} fusion(f32[6144,128]{1,0:T(8,128)S(1)} %get-tuple-element.23, f32[6144]{0:T(1024)S(1)} %add_rsqrt_fusion, f32[6144]{0:T(1024)S(1)} %broadcast_multiply_fusion), kind=kLoop, calls=%fused_computation.16 | loop fusion | flops 1572864 | bytes 6340608 | tf_op jit(solution)/shard_map/mul | solution.py:19
  93.0 0.4 add_reduce_fusion
  93.4 0.6 fusion.2
  94.0 0.6 fusion.69
  95.0 3.2 %scatter_custom_fusion.2 = f32[128,128]{1,0:T(8,128)S(1)} fusion(s32[1024]{0:T(1024)} %bitcast.87, f32[1024,128]{1,0:T(8,128)S(1)} %copy.47, f32[]{:T(128)} %constant.29.clone.1), kind=kCustom, calls=%fused_computation.79 | custom fusion | bytes 66048 | tf_op jit(solution)/shard_map/scatter | solution.py:101
  98.2 3.4 %scatter_custom_fusion.3 = f32[128,128]{1,0:T(8,128)S(1)} fusion(s32[1024]{0:T(1024)} %bitcast.85, f32[1024,128]{1,0:T(8,128)S(1)} %copy.47, f32[]{:T(128)} %constant.29.clone.1), kind=kCustom, calls=%fused_computation.77 | custom fusion | bytes 66048 | tf_op jit(solution)/shard_map/scatter | solution.py:101
  101.8 5.4 %collective-permute-start.4 = (f32[128,128]{0,1:T(8,128)S(1)}, f32[128,128]{0,1:T(8,128)S(1)}, u32[]{:S(2)}, u32[]{:S(2)}) collective-permute-start(f32[128,128]{0,1:T(8,128)S(1)} %copy.48), channel_id=1, source_target_pairs={{0,4},{4,8},{8,12},{12,16},{16,20},{20,24},{24,28},{28,32},{32,36}... | collective-permute-start | bytes 196616 | tf_op jit(solution)/shard_map/ppermute | solution.py:12
  107.3 1.9 %collective-permute-start.5 = (f32[128,128]{0,1:T(8,128)S(1)}, f32[128,128]{0,1:T(8,128)S(1)}, u32[]{:S(2)}, u32[]{:S(2)}) collective-permute-start(f32[128,128]{0,1:T(8,128)S(1)} %copy.50), channel_id=1, source_target_pairs={{4,0},{8,4},{12,8},{16,12},{20,16},{24,20},{28,24},{32,28},{36,32}... | collective-permute-start | bytes 196616 | tf_op jit(solution)/shard_map/ppermute | solution.py:12
  109.3 7.0 %collective-permute-done.5 = f32[128,128]{0,1:T(8,128)S(1)} collective-permute-done((f32[128,128]{0,1:T(8,128)S(1)}, f32[128,128]{0,1:T(8,128)S(1)}, u32[]{:S(2)}, u32[]{:S(2)}) %collective-permute-start.5) | collective-permute-done | bytes 65568 | tf_op jit(solution)/shard_map/ppermute | solution.py:12
  116.2 0.8 fusion.4
  117.0 0.7 gather_fusion.4
  117.7 1.9 %collective-permute-start.6 = (f32[64,128]{1,0:T(8,128)S(1)}, f32[64,128]{1,0:T(8,128)S(1)}, u32[]{:S(2)}, u32[]{:S(2)}) collective-permute-start(f32[64,128]{1,0:T(8,128)S(1)} %gather_fusion.4), channel_id=1, source_target_pairs={{0,4},{4,8},{8,12},{12,16},{16,20},{20,24},{24,28},{28,32},{32,36}... | collective-permute-start | bytes 98312 | tf_op jit(solution)/shard_map/ppermute | solution.py:12
  119.7 0.7 gather_fusion.5
  120.4 2.4 %collective-permute-start.7 = (f32[64,128]{1,0:T(8,128)S(1)}, f32[64,128]{1,0:T(8,128)S(1)}, u32[]{:S(2)}, u32[]{:S(2)}) collective-permute-start(f32[64,128]{1,0:T(8,128)S(1)} %gather_fusion.5), channel_id=1, source_target_pairs={{4,0},{8,4},{12,8},{16,12},{20,16},{24,20},{28,24},{32,28},{36,32}... | collective-permute-start | bytes 98312 | tf_op jit(solution)/shard_map/ppermute | solution.py:12
  122.8 0.3 fusion.36
  123.1 0.3 fusion.38
  123.4 5.6 %collective-permute-done.7 = f32[64,128]{1,0:T(8,128)S(1)} collective-permute-done((f32[64,128]{1,0:T(8,128)S(1)}, f32[64,128]{1,0:T(8,128)S(1)}, u32[]{:S(2)}, u32[]{:S(2)}) %collective-permute-start.7) | collective-permute-done | bytes 32800 | tf_op jit(solution)/shard_map/ppermute | solution.py:12
  128.9 0.3 fusion.21
  129.3 2.6 %gather_fusion.6 = f32[1536,128]{1,0:T(8,128)S(1)} fusion(f32[384,128]{1,0:T(8,128)S(1)} %fusion.21, s32[2048]{0:T(1024)S(1)} %pad_clamp_fusion), kind=kCustom, calls=%fused_computation.6 | custom fusion | bytes 1579008 | tf_op jit(solution)/shard_map/gather | solution.py:29
  132.0 0.9 fusion.70
  132.8 0.5 multiply_reduce_fusion.1
  133.3 0.5 subtract_multiply_fusion.1
  133.9 0.3 fusion.3
  134.2 0.3 fusion.71
  134.8 1.3 fusion
  136.1 1.9 %collective-permute-start.9 = (f32[128,128]{1,0:T(8,128)S(1)}, f32[128,128]{1,0:T(8,128)S(1)}, u32[]{:S(2)}, u32[]{:S(2)}) collective-permute-start(f32[128,128]{1,0:T(8,128)S(1)} %get-tuple-element.8), channel_id=1, source_target_pairs={{0,4},{4,8},{8,12},{12,16},{16,20},{20,24},{24,28},{28,32},{32,36}... | collective-permute-start | bytes 196616 | tf_op jit(solution)/shard_map/ppermute | solution.py:12
  138.0 2.4 %collective-permute-start.8 = (f32[128,128]{1,0:T(8,128)S(1)}, f32[128,128]{1,0:T(8,128)S(1)}, u32[]{:S(2)}, u32[]{:S(2)}) collective-permute-start(f32[128,128]{1,0:T(8,128)S(1)} %get-tuple-element.9), channel_id=1, source_target_pairs={{4,0},{8,4},{12,8},{16,12},{20,16},{24,20},{28,24},{32,28},{36,32}... | collective-permute-start | bytes 196616 | tf_op jit(solution)/shard_map/ppermute | solution.py:12
  140.5 0.2 copy.56
  140.7 2.8 %gather_fusion.8 = f32[1024,128]{1,0:T(8,128)S(1)} fusion(f32[128,128]{1,0:T(8,128)S(1)} %collective-permute-done.9, s32[1024]{0:T(1024)S(1)} %copy-done.11), kind=kCustom, calls=%fused_computation.8 | custom fusion | bytes 1052672 | tf_op jit(solution)/shard_map/gather | solution.py:140
  143.6 0.2 copy.53
  143.8 3.2 %collective-permute-done.8 = f32[128,128]{1,0:T(8,128)S(1)} collective-permute-done((f32[128,128]{1,0:T(8,128)S(1)}, f32[128,128]{1,0:T(8,128)S(1)}, u32[]{:S(2)}, u32[]{:S(2)}) %collective-permute-start.8) | collective-permute-done | bytes 65568 | tf_op jit(solution)/shard_map/ppermute | solution.py:12
  146.9 2.8 %gather_fusion.7 = f32[1024,128]{1,0:T(8,128)S(1)} fusion(f32[128,128]{1,0:T(8,128)S(1)} %collective-permute-done.8, s32[1024]{0:T(1024)S(1)} %broadcast_clamp_fusion.2), kind=kCustom, calls=%fused_computation.7 | custom fusion | bytes 1052672 | tf_op jit(solution)/shard_map/gather | solution.py:139
  150.2 1.0 copy.55
  (88 shorter events, 2.5 us)
Async XLA Ops:
  0.0 84.9 %copy-start = (f32[128,128]{1,0:T(8,128)S(1)}, f32[128,128]{1,0:T(8,128)}, u32[]{:S(2)}) copy-start(f32[128,128]{1,0:T(8,128)} %param.27) | copy-start | bytes 196612
  0.0 48.8 %copy-start.1 = (f32[1024,128]{1,0:T(8,128)S(1)}, f32[1024,128]{1,0:T(8,128)}, u32[]{:S(2)}) copy-start(f32[1024,128]{1,0:T(8,128)} %param.17) | copy-start | bytes 1572868
  0.0 48.7 %copy-start.10 = (s32[6,1024]{1,0:T(8,128)S(1)}, s32[6,1024]{1,0:T(8,128)}, u32[]{:S(2)}) copy-start(s32[6,1024]{1,0:T(8,128)} %param.19) | copy-start | bytes 73732
  0.0 48.8 %copy-start.3 = (f32[384,128]{1,0:T(8,128)S(1)}, f32[384,128]{1,0:T(8,128)}, u32[]{:S(2)}) copy-start(f32[384,128]{1,0:T(8,128)} %param.26) | copy-start | bytes 589828
  3.1 56.2 %collective-permute-start = (f32[96,128]{1,0:T(8,128)}, f32[96,128]{1,0:T(8,128)}, u32[]{:S(2)}, u32[]{:S(2)}) collective-permute-start(f32[96,128]{1,0:T(8,128)} %gather_fusion.1), channel_id=1, source_target_pairs={{0,4},{4,8},{8,12},{12,16},{16,20},{20,24},{24,28},{28,32},{32,36}... | collective-permute-start | bytes 147464 | tf_op jit(solution)/shard_map/ppermute | solution.py:12
  10.3 48.9 %collective-permute-start.1 = (f32[96,128]{1,0:T(8,128)}, f32[96,128]{1,0:T(8,128)}, u32[]{:S(2)}, u32[]{:S(2)}) collective-permute-start(f32[96,128]{1,0:T(8,128)} %gather_fusion.2), channel_id=1, source_target_pairs={{4,0},{8,4},{12,8},{16,12},{20,16},{24,20},{28,24},{32,28},{36,32}... | collective-permute-start | bytes 147464 | tf_op jit(solution)/shard_map/ppermute | solution.py:12
  15.4 33.4 %copy-start.16 = (s32[1024,1]{0,1:T(1,128)}, s32[1024,1]{0,1:T(1,128)S(1)}, u32[]{:S(2)}) copy-start(s32[1024,1]{0,1:T(1,128)S(1)} %get-tuple-element.12) | copy-start | bytes 12292
  15.4 39.6 %copy-start.15 = (s32[1024,1]{0,1:T(1,128)}, s32[1024,1]{0,1:T(1,128)S(1)}, u32[]{:S(2)}) copy-start(s32[1024,1]{0,1:T(1,128)S(1)} %get-tuple-element.11) | copy-start | bytes 12292
  20.9 36.7 %collective-permute-start.3 = (s32[128]{0:T(128)}, s32[128]{0:T(128)}, u32[]{:S(2)}, u32[]{:S(2)}) collective-permute-start(s32[128]{0:T(128)} %scatter_custom_fusion.1), channel_id=1, source_target_pairs={{4,0},{8,4},{12,8},{16,12},{20,16},{24,20},{28,24},{32,28},{36,32}... | collective-permute-start | bytes 1544 | tf_op jit(solution)/shard_map/ppermute | solution.py:12
  27.6 30.7 %collective-permute-start.2 = (s32[128]{0:T(128)}, s32[128]{0:T(128)}, u32[]{:S(2)}, u32[]{:S(2)}) collective-permute-start(s32[128]{0:T(128)} %scatter_custom_fusion), channel_id=1, source_target_pairs={{0,4},{4,8},{8,12},{12,16},{16,20},{20,24},{24,28},{28,32},{32,36}... | collective-permute-start | bytes 1544 | tf_op jit(solution)/shard_map/ppermute | solution.py:12
  49.4 5.6 %copy-start.4 = (f32[256,128]{1,0:T(8,128)S(1)}, f32[256,128]{1,0:T(8,128)}, u32[]{:S(2)}) copy-start(f32[256,128]{1,0:T(8,128)} %param.28) | copy-start | bytes 393220
  49.4 6.1 %copy-start.17 = (s32[1,2,64]{2,1,0:T(2,128)S(1)}, s32[1,2,64]{2,1,0:T(2,128)}, u32[]{:S(2)}) copy-start(s32[1,2,64]{2,1,0:T(2,128)} %param.25) | copy-start | bytes 1540
  49.4 6.7 %copy-start.12 = (s32[6,256]{1,0:T(8,128)S(1)}, s32[6,256]{1,0:T(8,128)}, u32[]{:S(2)}) copy-start(s32[6,256]{1,0:T(8,128)} %param.24) | copy-start | bytes 18436
  89.6 3.3 %copy-start.2 = (f32[6,1024,128]{2,1,0:T(8,128)S(1)}, f32[6,1024,128]{2,1,0:T(8,128)}, u32[]{:S(2)}) copy-start(f32[6,1024,128]{2,1,0:T(8,128)} %param.18) | copy-start | bytes 9437188
  92.9 1.0 copy-start.7
  94.6 28.2 %copy-start.5 = (f32[256,128]{1,0:T(8,128)S(1)}, f32[256,128]{1,0:T(8,128)}, u32[]{:S(2)}) copy-start(f32[256,128]{1,0:T(8,128)} %param.30) | copy-start | bytes 393220
  94.6 28.4 %copy-start.6 = (f32[256,128]{1,0:T(8,128)S(1)}, f32[256,128]{1,0:T(8,128)}, u32[]{:S(2)}) copy-start(f32[256,128]{1,0:T(8,128)} %param.32) | copy-start | bytes 393220
  101.8 7.5 %collective-permute-start.4 = (f32[128,128]{0,1:T(8,128)S(1)}, f32[128,128]{0,1:T(8,128)S(1)}, u32[]{:S(2)}, u32[]{:S(2)}) collective-permute-start(f32[128,128]{0,1:T(8,128)S(1)} %copy.48), channel_id=1, source_target_pairs={{0,4},{4,8},{8,12},{12,16},{16,20},{20,24},{24,28},{28,32},{32,36}... | collective-permute-start | bytes 196616 | tf_op jit(solution)/shard_map/ppermute | solution.py:12
  107.3 8.9 %collective-permute-start.5 = (f32[128,128]{0,1:T(8,128)S(1)}, f32[128,128]{0,1:T(8,128)S(1)}, u32[]{:S(2)}, u32[]{:S(2)}) collective-permute-start(f32[128,128]{0,1:T(8,128)S(1)} %copy.50), channel_id=1, source_target_pairs={{4,0},{8,4},{12,8},{16,12},{20,16},{24,20},{28,24},{32,28},{36,32}... | collective-permute-start | bytes 196616 | tf_op jit(solution)/shard_map/ppermute | solution.py:12
  117.7 5.6 %collective-permute-start.6 = (f32[64,128]{1,0:T(8,128)S(1)}, f32[64,128]{1,0:T(8,128)S(1)}, u32[]{:S(2)}, u32[]{:S(2)}) collective-permute-start(f32[64,128]{1,0:T(8,128)S(1)} %gather_fusion.4), channel_id=1, source_target_pairs={{0,4},{4,8},{8,12},{12,16},{16,20},{20,24},{24,28},{28,32},{32,36}... | collective-permute-start | bytes 98312 | tf_op jit(solution)/shard_map/ppermute | solution.py:12
  120.4 8.5 %collective-permute-start.7 = (f32[64,128]{1,0:T(8,128)S(1)}, f32[64,128]{1,0:T(8,128)S(1)}, u32[]{:S(2)}, u32[]{:S(2)}) collective-permute-start(f32[64,128]{1,0:T(8,128)S(1)} %gather_fusion.5), channel_id=1, source_target_pairs={{4,0},{8,4},{12,8},{16,12},{20,16},{24,20},{28,24},{32,28},{36,32}... | collective-permute-start | bytes 98312 | tf_op jit(solution)/shard_map/ppermute | solution.py:12
  129.2 2.7 %copy-start.8 = (f32[128,128]{1,0:T(8,128)S(1)}, f32[128,128]{1,0:T(8,128)}, u32[]{:S(2)}) copy-start(f32[128,128]{1,0:T(8,128)} %param.31) | copy-start | bytes 196612
  131.9 2.2 %copy-start.9 = (f32[128,128]{1,0:T(8,128)S(1)}, f32[128,128]{1,0:T(8,128)}, u32[]{:S(2)}) copy-start(f32[128,128]{1,0:T(8,128)} %param.33) | copy-start | bytes 196612
  133.3 7.4 %copy-start.11 = (s32[1024]{0:T(1024)S(1)}, s32[1024]{0:T(1024)}, u32[]{:S(2)}) copy-start(s32[1024]{0:T(1024)} %broadcast_clamp_fusion.1) | copy-start | bytes 12292
  136.1 4.6 %collective-permute-start.9 = (f32[128,128]{1,0:T(8,128)S(1)}, f32[128,128]{1,0:T(8,128)S(1)}, u32[]{:S(2)}, u32[]{:S(2)}) collective-permute-start(f32[128,128]{1,0:T(8,128)S(1)} %get-tuple-element.8), channel_id=1, source_target_pairs={{0,4},{4,8},{8,12},{12,16},{16,20},{20,24},{24,28},{28,32},{32,36}... | collective-permute-start | bytes 196616 | tf_op jit(solution)/shard_map/ppermute | solution.py:12
  138.0 8.9 %collective-permute-start.8 = (f32[128,128]{1,0:T(8,128)S(1)}, f32[128,128]{1,0:T(8,128)S(1)}, u32[]{:S(2)}, u32[]{:S(2)}) collective-permute-start(f32[128,128]{1,0:T(8,128)S(1)} %get-tuple-element.9), channel_id=1, source_target_pairs={{4,0},{8,4},{12,8},{16,12},{20,16},{24,20},{28,24},{32,28},{36,32}... | collective-permute-start | bytes 196616 | tf_op jit(solution)/shard_map/ppermute | solution.py:12
  143.8 6.2 %copy-start.13 = (pred[1024]{0:T(1024)(128)(4,1)S(1)}, pred[1024]{0:T(1024)(128)(4,1)}, u32[]{:S(2)}) copy-start(pred[1024]{0:T(1024)(128)(4,1)} %get-tuple-element.5) | copy-start | bytes 3076
  143.8 6.2 %copy-start.14 = (pred[1024]{0:T(1024)(128)(4,1)S(1)}, pred[1024]{0:T(1024)(128)(4,1)}, u32[]{:S(2)}) copy-start(pred[1024]{0:T(1024)(128)(4,1)} %get-tuple-element.7) | copy-start | bytes 3076
where the time goes:
time: 152 us; the launch traced here: 151 us
  local copies, waits for them, and re-layouts  56.3 us (37%)
  starting transfers between devices  31.7 us (21%)
  other arithmetic  18.7 us (12%)
  matrix products  16.7 us (11%)
  waiting for transfers between devices  15.7 us (10%)
  blocking collectives  11.2 us (7%)
    ppermute x10, starting transfers between devices, shifted_2(): return lax.ppermute(block, axis, route)  31.7 us
    gather x2, local copies, waits for them, and re-layouts, message_layer(): from_table[neighbours.reshape(-1)].reshape(degree, count_rows, features)  23.5 us
    ppermute x10, waiting for transfers between devices, shifted_2(): return lax.ppermute(block, axis, route)  15.7 us
    all_gather x1, blocking collectives, local(): everyone = lax.all_gather(packed[None], 'sub', axis=0, tiled=True)  11.2 us
    scatter x2, local copies, waits for them, and re-layouts, local(): jnp.zeros((capacity,), jnp.int32).at[destination]  9.6 us
    scatter x4, local copies, waits for them, and re-layouts, local(): jnp.zeros((capacity, features), jnp.float32).at[destination]  6.85 us
    dot_general x1, matrix products, message_layer(): jnp.dot(edge_latent.reshape(-1, features), edge_in[2 * features:], precis...  5.54 us
    gather x2, local copies, waits for them, and re-layouts, local(): beside.append(shifted_2(fine_nodes[dom_lists[column]], 'dom', offset))  4.51 us
  transfers between devices with their start and end apart: 10, of which 3 were waited for; matrix products, arithmetic and copies ran while one was open for 22% of the time, Pallas kernels for 0%

commit v1 on v0

v1 whole, which is shorter than its diff:
```python
import functools

import jax
import jax.numpy as jnp
from jax import lax
from jax.experimental import pallas as pl
from jax.experimental.pallas import tpu as pltpu
from jax.sharding import PartitionSpec as P

F32 = jnp.float32
BF16 = jnp.bfloat16
LANES = 128
VMEM = pltpu.VMEM
SMEM = pltpu.SMEM


def split(values):
    high = values.astype(BF16)
    low = (values - high.astype(F32)).astype(BF16)
    return high, low


def wide(values):
    return jnp.concatenate(split(values), axis=1)


def square(weight):
    row = jnp.concatenate(split(weight), axis=1)
    return jnp.concatenate([row, row], axis=0)


def centred(weight):
    return weight - jnp.mean(weight, axis=1, keepdims=True)


def fold(product):
    return product[:, :LANES] + product[:, LANES:]


def matmul(rows, weight_square):
    return fold(jnp.dot(wide(rows), weight_square, preferred_element_type=F32))


def pick(one_hot, table_wide):
    return fold(jnp.dot(one_hot, table_wide, preferred_element_type=F32))


def scaled(shifted):
    spread = jnp.mean(shifted * shifted, axis=-1, keepdims=True)
    return shifted * lax.rsqrt(spread + 1e-05)


def one_hot(condition):
    return jnp.where(condition, 1.0, 0.0).astype(BF16)


def iota(shape, axis):
    return lax.broadcasted_iota(jnp.int32, shape, axis).astype(F32)


def is_even():
    return lax.rem(lax.axis_index("dom"), 2) == 0


def copy_rows(source, index_of, target, start, count, unroll=8):
    def body(step, carry):
        base = pl.multiple_of(step * unroll, unroll)
        for offset in range(unroll):
            target[pl.ds(start + base + offset, 1), :] = source[
                pl.ds(index_of(base + offset), 1), :
            ]
        return carry

    lax.fori_loop(0, count // unroll, body, 0)


def pack_kernel(
    sub_send, dom_send, owner, slot, nodes, sibling_out, core_out, chip_out, select_out
):
    halo = sub_send.shape[2]
    even = is_even()
    towards_core = jnp.where(even, 0, 1)
    for sibling in range(sub_send.shape[1]):
        copy_rows(
            nodes, lambda i: sub_send[0, sibling, i], sibling_out.at[sibling], 0, halo
        )
    copy_rows(nodes, lambda i: dom_send[0, towards_core, i], core_out, 0, halo)
    copy_rows(nodes, lambda i: dom_send[0, 1 - towards_core, i], chip_out, 0, halo)
    step = owner[...] - lax.axis_index("dom")
    core_step = jnp.where(even, 1, -1)
    upper = one_hot(iota((LANES, LANES), 0) <= iota((LANES, LANES), 1))
    ranks = []
    for direction in (core_step, -core_step):
        chosen = jnp.where(step == direction, 1.0, 0.0)
        inside = jnp.dot(chosen.astype(BF16), upper, preferred_element_type=F32)
        total = jnp.broadcast_to(jnp.sum(chosen, axis=1, keepdims=True), chosen.shape)
        before = jnp.zeros_like(total)
        rows = lax.broadcasted_iota(jnp.int32, total.shape, 0)
        running = total
        for shift in (1, 2, 4):
            moved = pltpu.roll(running, shift, 0)
            running = running + jnp.where(rows >= shift, moved, 0.0)
        before = running - total
        ranks.append((step == direction, inside + before - 1.0))
    own_slot = slot[...].astype(F32)
    count = 2 * LANES
    select = jnp.where(
        ranks[0][0],
        ranks[0][1] + count,
        jnp.where(ranks[1][0], ranks[1][1] + (count + LANES), own_slot),
    )
    select_out[...] = select
    sent = jnp.zeros((8, 2 * LANES), F32)
    for block in range(8):
        place = one_hot(iota((2 * LANES, LANES), 0) == select[block : block + 1] - count)
        slots = jnp.broadcast_to(own_slot[block : block + 1] + 1.0, (8, LANES)).astype(BF16)
        sent = sent + lax.dot_general(
            slots, place, (((1,), (1,)), ((), ())), preferred_element_type=F32
        )
    core_out[pl.ds(halo, 8), :] = sent[:, :LANES]
    chip_out[pl.ds(halo, 8), :] = sent[:, LANES:]


def before_kernel(
    edges, nodes, edge_in, select, coarse_nbr, coarse_send,
    pre_out, table_out, columns_out, weights, own_part, stage,
):
    step = pl.program_id(0)
    features = LANES

    @pl.when(step == 0)
    def _():
        weights[...] = square(edge_in[2 * features :, :])
        node_rows = wide(nodes[...])
        own_part[...] = fold(
            jnp.dot(node_rows, square(edge_in[:features, :]), preferred_element_type=F32)
        )
        table_out[...] = fold(
            jnp.dot(
                node_rows, square(edge_in[features : 2 * features, :]), preferred_element_type=F32
            )
        )
        stage[...] = jnp.zeros_like(stage)
        stage[0:8, :] = select[...]
        stage[8:14, :] = coarse_nbr[:, :LANES].astype(F32)
        stage[16:22, :] = coarse_nbr[:, LANES:].astype(F32)
        stage[24:26, 0 : coarse_send.shape[2]] = coarse_send[0].astype(F32)
        columns_out[...] = stage[...].T

    degree, rows, _ = edges.shape
    part = own_part[pl.ds(pl.multiple_of(step * rows, rows), rows), :]
    product = matmul(edges[...].reshape(degree * rows, features), weights[...])
    pre_out[...] = product.reshape(degree, rows, features) + part[None]


def fine_kernel(
    nbr, pre, edges, nodes, own_table, siblings, core_rows, chip_rows, select,
    edge_in, edge_out, node_in, node_out,
    mid_out, core_out, chip_out, sums_out, share_out, meta_out,
    table, gathered, weight_out, weight_self, weight_sum, weight_last, mid_wide, meta,
):
    step = pl.program_id(0)
    steps = pl.num_programs(0)
    features = LANES
    degree, rows, _ = edges.shape
    halo = siblings.shape[1]
    own = own_table.shape[0]
    other = core_rows.shape[0] // 2
    even = is_even()

    @pl.when(step == 0)
    def _():
        weight_out[...] = square(centred(edge_out[...]))
        weight_self[...] = square(node_in[:features, :])
        weight_sum[...] = square(node_in[features:, :])
        weight_last[...] = square(centred(node_out[...]))
        to_table = square(edge_in[features : 2 * features, :])
        table[0:own, :] = own_table[...]
        table[own : own + 4 * halo, :] = matmul(
            siblings[...].reshape(4 * halo, features), to_table
        )
        core_at = pl.multiple_of(jnp.where(even, other, 0), 8)
        core_block = core_rows[pl.ds(core_at, other), :]
        chip_block = chip_rows[...]
        halo_at = own + 4 * halo
        core_to = pl.multiple_of(halo_at + jnp.where(even, halo, 0), 8)
        chip_to = pl.multiple_of(halo_at + jnp.where(even, 0, halo), 8)
        table[pl.ds(core_to, halo), :] = matmul(core_block[:halo], to_table)
        table[pl.ds(chip_to, halo), :] = matmul(chip_block[:halo], to_table)
        meta[...] = jnp.zeros_like(meta)
        meta[0:1, :] = core_block[halo : halo + 1] - 1.0
        meta[1:2, :] = chip_block[halo : halo + 1] - 1.0

    first = pl.multiple_of(step * rows, rows)

    def gather(group, carry):
        base = pl.multiple_of(group * 8, 8)
        for slot in range(degree):
            for offset in range(8):
                index = nbr[slot, first + base + offset]
                gathered[slot, pl.ds(base + offset, 1), :] = table[pl.ds(index, 1), :]
        return carry

    lax.fori_loop(0, rows // 8, gather, 0)
    hidden = jnp.maximum(pre[...] + gathered[...], 0.0).reshape(degree * rows, features)
    message = scaled(matmul(hidden, weight_out[...])).reshape(degree, rows, features)
    summed = jnp.sum(edges[...] + message, axis=0)
    own_rows = nodes[...]
    node_hidden = jnp.maximum(
        matmul(own_rows, weight_self[...]) + matmul(summed, weight_sum[...]), 0.0
    )
    mid = own_rows + scaled(matmul(node_hidden, weight_last[...]))
    mid_out[...] = mid
    mid_wide[pl.ds(first, rows), :] = wide(mid)

    @pl.when(step == steps - 1)
    def _():
        coarse = sums_out.shape[0]
        total = jnp.zeros((2 * coarse, 2 * LANES), F32)
        count = jnp.zeros((coarse, LANES), F32)
        places = iota((2 * coarse, LANES), 0)
        for block in range(select.shape[0]):
            place = jnp.where(places == select[block : block + 1, :], 1.0, 0.0)
            count = count + place[:coarse]
            total = total + jnp.dot(
                place.astype(BF16),
                mid_wide[block * LANES : (block + 1) * LANES, :],
                preferred_element_type=F32,
            )
        total = fold(total)
        sums_out[...] = total[:coarse]
        core_out[...] = total[coarse : coarse + LANES]
        chip_out[...] = total[coarse + LANES :]
        for source in range(2):
            count = count + jnp.where(places[:coarse] == meta[source : source + 1, :], 1.0, 0.0)
        members = jnp.maximum(jnp.sum(count, axis=1, keepdims=True), 1.0)
        share_out[...] = jnp.broadcast_to(1.0 / members, (coarse, LANES))
        meta_out[0:8, :] = meta[0:8, :]
        meta_out[8 : 8 + LANES, :] = meta[...].T


def pool_kernel(sums, share, meta, columns, core_rows, chip_rows, pooled_out, core_out, chip_out):
    coarse = sums.shape[0]
    even = is_even()
    other = core_rows.shape[0] // 2
    core_block = core_rows[pl.ds(pl.multiple_of(jnp.where(even, other, 0), 8), other), :]
    received = wide(jnp.concatenate([core_block, chip_rows[...]], axis=0))
    places = iota((coarse, LANES), 0)
    member = jnp.concatenate(
        [one_hot(places == meta[0:1, :]), one_hot(places == meta[1:2, :])], axis=1
    )
    pooled = (sums[...] + pick(member, received)) * share[...]
    pooled_out[...] = pooled
    pooled_wide = wide(pooled)
    rows = core_out.shape[0]
    lanes = iota((rows, coarse), 1)
    next_rows = pick(one_hot(lanes == columns[0:rows, 24:25]), pooled_wide)
    prev_rows = pick(one_hot(lanes == columns[0:rows, 25:26]), pooled_wide)
    core_out[...] = jnp.where(even, next_rows, prev_rows)
    chip_out[...] = jnp.where(even, prev_rows, next_rows)


def coarse_kernel(
    pooled_in, meta, columns, core_rows, chip_rows, edge_in, edge_out, node_in, node_out,
    refined_out, core_out, chip_out, table,
):
    features = LANES
    even = is_even()
    pooled = pooled_in[...]
    coarse = pooled.shape[0]
    other = core_rows.shape[0] // 2
    core_block = core_rows[pl.ds(pl.multiple_of(jnp.where(even, other, 0), 8), other), :]
    chip_block = chip_rows[...]
    to_table = square(edge_in[features:, :])
    prev_rows = jnp.where(even, chip_block, core_block)
    next_rows = jnp.where(even, core_block, chip_block)
    extended = jnp.concatenate([pooled, prev_rows, next_rows], axis=0)
    table[...] = wide(matmul(extended, to_table))
    from_own = matmul(pooled, square(edge_in[:features, :]))
    weight_out = square(centred(edge_out[...]))
    extent = extended.shape[0]
    lanes = iota((LANES, extent), 1)
    degree = 6
    summed = []
    for block in range(coarse // LANES):
        hot = jnp.concatenate(
            [
                one_hot(lanes == columns[:, 8 + 8 * block + slot : 9 + 8 * block + slot])
                for slot in range(degree)
            ],
            axis=0,
        )
        near = pick(hot, table[...]).reshape(degree, LANES, features)
        own = from_own[block * LANES : (block + 1) * LANES]
        hidden = jnp.maximum(near + own[None], 0.0).reshape(degree * LANES, features)
        message = scaled(matmul(hidden, weight_out)).reshape(degree, LANES, features)
        summed.append(jnp.sum(message, axis=0))
    total = jnp.concatenate(summed, axis=0)
    node_hidden = jnp.maximum(
        matmul(pooled, square(node_in[:features, :])) + matmul(total, square(node_in[features:, :])),
        0.0,
    )
    refined = pooled + scaled(matmul(node_hidden, square(centred(node_out[...]))))
    refined_out[...] = refined
    refined_wide = wide(refined)
    slots = iota((LANES, coarse), 1)
    core_out[...] = pick(one_hot(slots == meta[8 : 8 + LANES, 0:1]), refined_wide)
    chip_out[...] = pick(one_hot(slots == meta[8 : 8 + LANES, 1:2]), refined_wide)


def last_kernel(mid, refined, columns, core_rows, chip_rows, out, table):
    even = is_even()
    coarse = refined.shape[0]
    other = core_rows.shape[0] // 2
    core_block = core_rows[pl.ds(pl.multiple_of(jnp.where(even, other, 0), 8), other), :]
    table[0:coarse, :] = wide(refined[...])
    table[coarse : coarse + other, :] = wide(core_block)
    table[coarse + other :, :] = wide(chip_rows[...])
    lanes = iota((LANES, coarse + 2 * other), 1)
    for block in range(mid.shape[0] // LANES):
        rows = slice(block * LANES, (block + 1) * LANES)
        hot = one_hot(lanes == columns[:, block : block + 1])
        out[rows, :] = mid[rows, :] + pick(hot, table[...])


def shape(*dims):
    return jax.ShapeDtypeStruct(dims, F32)


def call(kernel, outs, args, places, scratch=(), grid=(), out_specs=None, flops=0, bytes_=0, vmem=None):
    whole = {"v": pl.BlockSpec(memory_space=VMEM), "s": pl.BlockSpec(memory_space=SMEM)}
    specs = [whole[p] if isinstance(p, str) else p for p in places]
    if out_specs is None:
        out_specs = [whole["v"]] * len(outs)
    return pl.pallas_call(
        kernel,
        out_shape=outs,
        grid=grid,
        in_specs=specs,
        out_specs=out_specs,
        scratch_shapes=list(scratch),
        cost_estimate=pl.CostEstimate(flops=flops, bytes_accessed=bytes_, transcendentals=0),
        compiler_params=pltpu.CompilerParams(vmem_limit_bytes=vmem or 32 * 2**20),
    )(*args)


def over_core(block):
    size = lax.axis_size("dom")
    groups = [[i, i + 1] for i in range(0, size, 2)]
    return lax.all_gather(block, "dom", axis=0, tiled=True, axis_index_groups=groups)


def over_chip(block):
    size = lax.axis_size("dom")
    route = []
    for i in range(1, size - 1, 2):
        route += [(i, i + 1), (i + 1, i)]
    return lax.ppermute(block, "dom", route)


def local(
    fine_nodes, fine_edges, fine_nbr, sub_send, dom_send, pool_owner, pool_slot, coarse_nbr,
    coarse_send, fine_edge_in, fine_edge_out, fine_node_in, fine_node_out, coarse_edge_in,
    coarse_edge_out, coarse_node_in, coarse_node_out,
):
    node_rows, features = fine_nodes.shape
    degree = fine_nbr.shape[0]
    coarse = coarse_nbr.shape[1]
    halo = sub_send.shape[2]
    coarse_halo = coarse_send.shape[2]
    capacity = node_rows // 8
    extent = node_rows + 6 * halo
    owner = pool_owner[:, 0].reshape(8, LANES)
    slot = pool_slot.reshape(8, LANES)

    sibling_send, core_send, chip_send, select = call(
        pack_kernel,
        [shape(4, halo, features), shape(halo + 8, features), shape(halo + 8, features), shape(8, LANES)],
        [sub_send, dom_send, owner, slot, fine_nodes],
        "ssvvv",
    )
    siblings = lax.all_to_all(sibling_send, "sub", 0, 0)
    chip_rows = over_chip(chip_send)
    core_rows = over_core(core_send)

    rows = LANES
    steps = node_rows // rows
    edge_block = pl.BlockSpec((degree, rows, features), lambda i: (0, i, 0))
    node_block = pl.BlockSpec((rows, features), lambda i: (i, 0))

    def fixed(*dims):
        return pl.BlockSpec(dims, lambda i: (0,) * len(dims))

    pre, own_table, columns = call(
        before_kernel,
        [shape(degree, node_rows, features), shape(node_rows, features), shape(LANES, LANES)],
        [fine_edges, fine_nodes, fine_edge_in, select, coarse_nbr, coarse_send],
        [
            edge_block, fixed(node_rows, features), fixed(3 * features, features),
            fixed(8, LANES), fixed(degree, coarse), fixed(1, 2, coarse_halo),
        ],
        scratch=[VMEM((256, 256), BF16), VMEM((node_rows, features), F32), VMEM((LANES, LANES), F32)],
        grid=(steps,),
        out_specs=[edge_block, fixed(node_rows, features), fixed(LANES, LANES)],
        flops=2 * 8192 * 128 * 128 * 6,
        bytes_=6291456,
    )
    weight = VMEM((256, 256), BF16)
    mid, core_send, chip_send, sums, share, meta = call(
        fine_kernel,
        [
            shape(node_rows, features), shape(capacity, features), shape(capacity, features),
            shape(coarse, features), shape(coarse, LANES), shape(8 + LANES, LANES),
        ],
        [
            fine_nbr, pre, fine_edges, fine_nodes, own_table, siblings, core_rows, chip_rows,
            select, fine_edge_in, fine_edge_out, fine_node_in, fine_node_out,
        ],
        [
            "s", edge_block, edge_block, node_block, fixed(node_rows, features),
            fixed(4, halo, features), fixed(2 * (halo + 8), features), fixed(halo + 8, features),
            fixed(8, LANES), fixed(3 * features, features), fixed(features, features),
            fixed(2 * features, features), fixed(features, features),
        ],
        scratch=[
            VMEM((extent, features), F32), VMEM((degree, rows, features), F32),
            weight, weight, weight, weight, VMEM((node_rows, 2 * LANES), BF16),
            VMEM((LANES, LANES), F32),
        ],
        grid=(steps,),
        out_specs=[
            node_block, fixed(capacity, features), fixed(capacity, features),
            fixed(coarse, features), fixed(coarse, LANES), fixed(8 + LANES, LANES),
        ],
        flops=2 * 8192 * 128 * 128 * 12,
        bytes_=8 * 2**20,
    )
    chip_rows = over_chip(chip_send)
    core_rows = over_core(core_send)
    pooled, core_send, chip_send = call(
        pool_kernel,
        [shape(coarse, features), shape(coarse_halo, features), shape(coarse_halo, features)],
        [sums, share, meta, columns, core_rows, chip_rows],
        "vvvvvv",
    )
    chip_rows = over_chip(chip_send)
    core_rows = over_core(core_send)
    refined, core_send, chip_send = call(
        coarse_kernel,
        [shape(coarse, features), shape(capacity, features), shape(capacity, features)],
        [
            pooled, meta, columns, core_rows, chip_rows,
            coarse_edge_in, coarse_edge_out, coarse_node_in, coarse_node_out,
        ],
        "vvvvvvvvv",
        scratch=[VMEM((coarse + 2 * coarse_halo, 2 * LANES), BF16)],
    )
    chip_rows = over_chip(chip_send)
    core_rows = over_core(core_send)
    (out,) = call(
        last_kernel,
        [shape(node_rows, features)],
        [mid, refined, columns, core_rows, chip_rows],
        "vvvvv",
        scratch=[VMEM((coarse + 2 * capacity, 2 * LANES), BF16)],
    )
    return out


def solution(mesh):
    rows = P(("dom", "sub"))
    slots = P(None, ("dom", "sub"))
    in_specs = (rows, slots, slots, rows, rows, rows, rows, slots, rows) + (P(),) * 8
    return jax.shard_map(local, mesh=mesh, in_specs=in_specs, out_specs=rows, check_vma=False)
```

time: 152 us -> 80.8 us (0.53)
  the two profiles are of different devices: /device:TPU:255 before, /device:TPU:251 now
where the time goes in v1:
time: 80.8 us; the launch traced here: 80.1 us
  Pallas kernels  27.4 us (34%)
  starting transfers between devices  20 us (25%)
  local copies, waits for them, and re-layouts  14.4 us (18%)
  waiting for transfers between devices  10.7 us (13%)
  blocking collectives  7.52 us (9%)
    pallas_call x6, Pallas kernels, call(): pl.pallas_call(kernel, out_shape=outs, grid=grid, in_specs=specs, out_spe...  27.4 us
    ppermute x4, starting transfers between devices, over_chip(): return lax.ppermute(block, 'dom', route)  15.6 us
    unnamed x46, local copies, waits for them, and re-layouts  14.4 us
    ppermute x4, waiting for transfers between devices, over_chip(): return lax.ppermute(block, 'dom', route)  10.7 us
    all_gather x4, blocking collectives, over_core(): lax.all_gather(block, 'dom', axis=0, tiled=True, axis_index_groups=groups)  7.52 us
    all_to_all x1, starting transfers between devices, local(): siblings = lax.all_to_all(sibling_send, 'sub', 0, 0)  4.4 us
  transfers between devices with their start and end apart: 5, of which 3 were waited for; matrix products, arithmetic and copies ran while one was open for 0% of the time, Pallas kernels for 4%

profile of v1, /device:TPU:251, one launch (start us, length us, event | category | flops | bytes accessed | tf_op | source)
XLA Modules:
  0.0 80.1 jit_solution(8846255451099198016)
XLA Ops:
  0.0 0.0 copy-start
  0.0 1.0 %copy-done = f32[1024,128]{1,0:T(8,128)S(1)} copy-done((f32[1024,128]{1,0:T(8,128)S(1)}, f32[1024,128]{1,0:T(8,128)}, u32[]{:S(2)}) %copy-start) | copy-done | bytes 524312
  1.0 0.0 copy-start.7
  1.0 0.7 copy-done.7
  1.7 0.0 copy-start.8
  1.7 0.7 copy-done.8
  2.4 0.0 copy-start.9
  2.4 0.7 copy-done.9
  3.1 0.0 copy-start.10
  3.1 0.7 copy-done.10
  3.8 2.7 %shard_map.163 = (f32[4,96,128]{2,1,0:T(8,128)}, f32[104,128]{1,0:T(8,128)S(1)}, f32[104,128]{1,0:T(8,128)S(1)}, f32[8,128]{1,0:T(8,128)S(1)}) custom-call(s32[1,4,96]{2,1,0:T(4,128)S(1)} %copy-done.9, s32[1,2,96]{2,1,0:T(2,128)S(1)} %copy-done.10, s32[8,128]{1,0:T(8,128)S(1)} %bitcast.2, s32[8,128]{1,0:T(8,128)S(1)} %bitcast.3, f32[1024,128]{1,0:T(8,128)S(1)} %copy-done), custom_call_target="tpu_custom_call" | custom-call | tf_op jit(solution)/shard_map/pallas_call | solution.py:335
  6.5 0.0 copy-start.14
  6.5 0.0 copy-start.15
  6.5 0.0 copy-start.16
  6.5 4.4 %all-to-all-start = ((f32[4,96,128]{2,1,0:T(8,128)}), f32[4,96,128]{2,1,0:T(8,128)S(1)}, u32[]{:S(2)}, u32[]{:S(2)}) async-start(f32[4,96,128]{2,1,0:T(8,128)} %get-tuple-element.27), calls=%async_computation | async-start | bytes 393216 | tf_op jit(solution)/shard_map/all_to_all | solution.py:382
  10.9 5.5 %collective-permute-start = (f32[104,128]{1,0:T(8,128)S(1)}, f32[104,128]{1,0:T(8,128)S(1)}, u32[]{:S(2)}, u32[]{:S(2)}) collective-permute-start(f32[104,128]{1,0:T(8,128)S(1)} %get-tuple-element.29), channel_id=1, source_target_pairs={{4,8},{8,4},{12,16},{16,12},{20,24},{24,20},{28,32},{32,28},{36,40... | collective-permute-start | bytes 159752 | tf_op jit(solution)/shard_map/ppermute | solution.py:358
  16.4 0.0 copy-start.1
  16.5 1.0 %copy-done.1 = f32[1024,128]{1,0:T(8,128)S(1)} copy-done((f32[1024,128]{1,0:T(8,128)S(1)}, f32[1024,128]{1,0:T(8,128)}, u32[]{:S(2)}) %copy-start.1) | copy-done | bytes 524312
  17.5 1.9 %copy-done.11 = f32[6,1024,128]{2,1,0:T(8,128)S(1)} copy-done((f32[6,1024,128]{2,1,0:T(8,128)S(1)}, f32[6,1024,128]{2,1,0:T(8,128)}, u32[]{:S(2)}) %copy-start.11) | copy-done | bytes 3145752
  19.4 0.9 %copy-done.13 = f32[384,128]{1,0:T(8,128)S(1)} copy-done((f32[384,128]{1,0:T(8,128)S(1)}, f32[384,128]{1,0:T(8,128)}, u32[]{:S(2)}) %copy-start.13) | copy-done | bytes 196632
  20.3 0.0 copy-start.19
  20.3 0.7 copy-done.19
  21.0 0.0 copy-start.20
  21.0 0.7 copy-done.20
  21.7 0.0 copy-start.2
  21.7 0.0 copy-start.17
  21.7 0.0 copy-start.18
  21.7 3.2 %shard_map.164 = (f32[6,1024,128]{2,1,0:T(8,128)S(1)}, f32[1024,128]{1,0:T(8,128)S(1)}, f32[128,128]{1,0:T(8,128)S(1)}) custom-call(f32[6,1024,128]{2,1,0:T(8,128)S(1)} %copy-done.11, f32[1024,128]{1,0:T(8,128)S(1)} %copy-done.1, f32[384,128]{1,0:T(8,128)S(1)} %copy-done.13, f32[8,128]{1,0:T(8,128)S(1)} %get-tuple-element.24.select, ...), custom_call_target="tpu_custom_call" | custom-call | flops 1610612736 | bytes 6291456 | tf_op jit(solution)/shard_map/pallas_call | solution.py:335
  24.9 0.0 copy-start.21
  24.9 1.6 %copy-done.21 = f32[6,1024,128]{2,1,0:T(8,128)} copy-done((f32[6,1024,128]{2,1,0:T(8,128)}, f32[6,1024,128]{2,1,0:T(8,128)S(1)}, u32[]{:S(2)}) %copy-start.21) | copy-done | bytes 3145752
  26.5 1.9 %all_gather.12.core_rows = f32[208,128]{1,0:T(8,128)S(1)} all-gather(f32[104,128]{1,0:T(8,128)S(1)} %get-tuple-element.28), channel_id=1, replica_groups={{0,4},{8,12},{16,20},{24,28},{32,36},{40,44},{48,52},{56,60},{64,68},{7..., dimensions={0}, use_global_device_ids=true | all-gather | bytes 159744 | tf_op jit(solution)/shard_map/all_gather | solution.py:350
  28.4 0.0 collective-permute-done.chip_rows
  28.4 0.0 all-to-all-done.siblings
  28.4 0.0 copy-done.14
  28.4 0.0 copy-done.15
  28.4 0.0 copy-done.16
  28.4 0.0 copy-done.2
  28.4 0.0 copy-done.17
  28.4 0.0 copy-done.18
  28.5 0.0 copy-start.12
  28.5 1.9 %copy-done.12 = f32[6,1024,128]{2,1,0:T(8,128)S(1)} copy-done((f32[6,1024,128]{2,1,0:T(8,128)S(1)}, f32[6,1024,128]{2,1,0:T(8,128)}, u32[]{:S(2)}) %copy-start.12) | copy-done | bytes 3145752
  30.3 0.0 copy-start.22
  30.4 1.9 %copy-done.22 = f32[6,1024,128]{2,1,0:T(8,128)S(1)} copy-done((f32[6,1024,128]{2,1,0:T(8,128)S(1)}, f32[6,1024,128]{2,1,0:T(8,128)}, u32[]{:S(2)}) %copy-start.22) | copy-done | bytes 3145752
  32.2 0.0 copy-start.3
  32.2 0.0 copy-start.4
  32.2 0.0 copy-start.5
  32.2 0.0 copy-start.6
  32.2 17.7 %shard_map.165 = (f32[1024,128]{1,0:T(8,128)S(1)}, f32[128,128]{1,0:T(8,128)S(1)}, f32[128,128]{1,0:T(8,128)S(1)}, f32[256,128]{1,0:T(8,128)S(1)}, f32[256,128]{1,0:T(8,128)S(1)}, /*index=5*/f32[136,128]{1,0:T(8,128)S(1)}) custom-call(s32[6,1024]{1,0:T(8,128)S(1)} %copy-done.18, f32[6,1024,128]{2,1,0:T(8,128)S(1)} %copy-done.22, ...), custom_call_target="tpu_custom_call" | custom-call | flops 3221225472 | bytes 8388608 | tf_op jit(solution)/shard_map/pallas_call | solution.py:335
  50.0 3.3 %collective-permute-start.1 = (f32[128,128]{1,0:T(8,128)S(1)}, f32[128,128]{1,0:T(8,128)S(1)}, u32[]{:S(2)}, u32[]{:S(2)}) collective-permute-start(f32[128,128]{1,0:T(8,128)S(1)} %get-tuple-element.36), channel_id=1, source_target_pairs={{4,8},{8,4},{12,16},{16,12},{20,24},{24,20},{28,32},{32,28},{36,40... | collective-permute-start | bytes 196616 | tf_op jit(solution)/shard_map/ppermute | solution.py:358
  53.4 1.9 %all_gather.13.core_rows = f32[256,128]{1,0:T(8,128)S(1)} all-gather(f32[128,128]{1,0:T(8,128)S(1)} %get-tuple-element.35), channel_id=1, replica_groups={{0,4},{8,12},{16,20},{24,28},{32,36},{40,44},{48,52},{56,60},{64,68},{7..., dimensions={0}, use_global_device_ids=true | all-gather | bytes 196608 | tf_op jit(solution)/shard_map/all_gather | solution.py:350
  55.3 3.7 %collective-permute-done.1.chip_rows = f32[128,128]{1,0:T(8,128)S(1)} collective-permute-done((f32[128,128]{1,0:T(8,128)S(1)}, f32[128,128]{1,0:T(8,128)S(1)}, u32[]{:S(2)}, u32[]{:S(2)}) %collective-permute-start.1) | collective-permute-done | bytes 65568 | tf_op jit(solution)/shard_map/ppermute | solution.py:358
  58.9 0.4 shard_map.166
  59.3 3.3 %collective-permute-start.2 = (f32[64,128]{1,0:T(8,128)S(1)}, f32[64,128]{1,0:T(8,128)S(1)}, u32[]{:S(2)}, u32[]{:S(2)}) collective-permute-start(f32[64,128]{1,0:T(8,128)S(1)} %get-tuple-element.39), channel_id=1, source_target_pairs={{4,8},{8,4},{12,16},{16,12},{20,24},{24,20},{28,32},{32,28},{36,40... | collective-permute-start | bytes 98312 | tf_op jit(solution)/shard_map/ppermute | solution.py:358
  62.7 1.9 %all_gather.14.core_rows = f32[128,128]{1,0:T(8,128)S(1)} all-gather(f32[64,128]{1,0:T(8,128)S(1)} %get-tuple-element.38), channel_id=1, replica_groups={{0,4},{8,12},{16,20},{24,28},{32,36},{40,44},{48,52},{56,60},{64,68},{7..., dimensions={0}, use_global_device_ids=true | all-gather | bytes 98304 | tf_op jit(solution)/shard_map/all_gather | solution.py:350
  64.5 3.3 %collective-permute-done.2.chip_rows = f32[64,128]{1,0:T(8,128)S(1)} collective-permute-done((f32[64,128]{1,0:T(8,128)S(1)}, f32[64,128]{1,0:T(8,128)S(1)}, u32[]{:S(2)}, u32[]{:S(2)}) %collective-permute-start.2) | collective-permute-done | bytes 32800 | tf_op jit(solution)/shard_map/ppermute | solution.py:358
  67.9 0.0 copy-done.3
  67.9 0.0 copy-done.4
  67.9 0.0 copy-done.5
  67.9 0.0 copy-done.6
  67.9 2.0 %shard_map.167 = (f32[256,128]{1,0:T(8,128)S(1)}, f32[128,128]{1,0:T(8,128)S(1)}, f32[128,128]{1,0:T(8,128)S(1)}) custom-call(f32[256,128]{1,0:T(8,128)S(1)} %get-tuple-element.37.pooled_in, f32[136,128]{1,0:T(8,128)S(1)} %get-tuple-element.33.meta, f32[128,128]{1,0:T(8,128)S(1)} %get-tuple-element.34.columns, f32[128,128]{1,0:T(8,128)S(1)} %all_gather.14.core_rows, ...), custom_call_target="tpu_custom_call" | custom-call | tf_op jit(solution)/shard_map/pallas_call | solution.py:335
  69.9 3.3 %collective-permute-start.3 = (f32[128,128]{1,0:T(8,128)S(1)}, f32[128,128]{1,0:T(8,128)S(1)}, u32[]{:S(2)}, u32[]{:S(2)}) collective-permute-start(f32[128,128]{1,0:T(8,128)S(1)} %get-tuple-element.42), channel_id=1, source_target_pairs={{4,8},{8,4},{12,16},{16,12},{20,24},{24,20},{28,32},{32,28},{36,40... | collective-permute-start | bytes 196616 | tf_op jit(solution)/shard_map/ppermute | solution.py:358
  73.3 1.9 %all_gather.15.core_rows = f32[256,128]{1,0:T(8,128)S(1)} all-gather(f32[128,128]{1,0:T(8,128)S(1)} %get-tuple-element.41), channel_id=1, replica_groups={{0,4},{8,12},{16,20},{24,28},{32,36},{40,44},{48,52},{56,60},{64,68},{7..., dimensions={0}, use_global_device_ids=true | all-gather | bytes 196608 | tf_op jit(solution)/shard_map/all_gather | solution.py:350
  75.2 3.7 %collective-permute-done.3.chip_rows = f32[128,128]{1,0:T(8,128)S(1)} collective-permute-done((f32[128,128]{1,0:T(8,128)S(1)}, f32[128,128]{1,0:T(8,128)S(1)}, u32[]{:S(2)}, u32[]{:S(2)}) %collective-permute-start.3) | collective-permute-done | bytes 65568 | tf_op jit(solution)/shard_map/ppermute | solution.py:358
  78.8 1.3 %shard_map.168 = f32[1024,128]{1,0:T(8,128)} custom-call(f32[1024,128]{1,0:T(8,128)S(1)} %get-tuple-element.30.mid, f32[256,128]{1,0:T(8,128)S(1)} %get-tuple-element.40.refined, f32[128,128]{1,0:T(8,128)S(1)} %get-tuple-element.34.columns, f32[256,128]{1,0:T(8,128)S(1)} %all_gather.15.core_rows, f32[128,128]{1,0:T(8,128)S(1)} %collective-permute-done.3.chip_rows), custom_call_target="tpu_custom_call" | custom-call | tf_op jit(solution)/shard_map/pallas_call | solution.py:335
  (2 shorter events, 0.0 us)
Async XLA Ops:
  0.0 1.0 %copy-start = (f32[1024,128]{1,0:T(8,128)S(1)}, f32[1024,128]{1,0:T(8,128)}, u32[]{:S(2)}) copy-start(f32[1024,128]{1,0:T(8,128)} %nodes.5) | copy-start | bytes 1572868
  1.0 0.7 copy-start.7
  1.7 0.7 copy-start.8
  2.4 0.7 copy-start.9
  3.1 0.7 copy-start.10
  6.5 21.9 %copy-start.14 = (f32[384,128]{1,0:T(8,128)S(1)}, f32[384,128]{1,0:T(8,128)}, u32[]{:S(2)}) copy-start(f32[384,128]{1,0:T(8,128)} %edge_in.4) | copy-start | bytes 589828
  6.5 21.9 %copy-start.15 = (f32[256,128]{1,0:T(8,128)S(1)}, f32[256,128]{1,0:T(8,128)}, u32[]{:S(2)}) copy-start(f32[256,128]{1,0:T(8,128)} %node_in.2) | copy-start | bytes 393220
  6.5 21.9 %copy-start.16 = (f32[128,128]{1,0:T(8,128)S(1)}, f32[128,128]{1,0:T(8,128)}, u32[]{:S(2)}) copy-start(f32[128,128]{1,0:T(8,128)} %edge_out.2) | copy-start | bytes 196612
  6.5 21.9 %all-to-all-start = ((f32[4,96,128]{2,1,0:T(8,128)}), f32[4,96,128]{2,1,0:T(8,128)S(1)}, u32[]{:S(2)}, u32[]{:S(2)}) async-start(f32[4,96,128]{2,1,0:T(8,128)} %get-tuple-element.27), calls=%async_computation | async-start | bytes 393216 | tf_op jit(solution)/shard_map/all_to_all | solution.py:382
  10.9 17.5 %collective-permute-start = (f32[104,128]{1,0:T(8,128)S(1)}, f32[104,128]{1,0:T(8,128)S(1)}, u32[]{:S(2)}, u32[]{:S(2)}) collective-permute-start(f32[104,128]{1,0:T(8,128)S(1)} %get-tuple-element.29), channel_id=1, source_target_pairs={{4,8},{8,4},{12,16},{16,12},{20,24},{24,20},{28,32},{32,28},{36,40... | collective-permute-start | bytes 159752 | tf_op jit(solution)/shard_map/ppermute | solution.py:358
  16.4 1.0 %copy-start.1 = (f32[1024,128]{1,0:T(8,128)S(1)}, f32[1024,128]{1,0:T(8,128)}, u32[]{:S(2)}) copy-start(f32[1024,128]{1,0:T(8,128)} %nodes.5) | copy-start | bytes 1572868
  17.5 1.9 %copy-start.11 = (f32[6,1024,128]{2,1,0:T(8,128)S(1)}, f32[6,1024,128]{2,1,0:T(8,128)}, u32[]{:S(2)}) copy-start(f32[6,1024,128]{2,1,0:T(8,128)} %edges.3) | copy-start | bytes 9437188
  19.4 0.9 %copy-start.13 = (f32[384,128]{1,0:T(8,128)S(1)}, f32[384,128]{1,0:T(8,128)}, u32[]{:S(2)}) copy-start(f32[384,128]{1,0:T(8,128)} %edge_in.4) | copy-start | bytes 589828
  20.3 0.7 copy-start.19
  21.0 0.7 copy-start.20
  21.7 6.7 %copy-start.2 = (f32[1024,128]{1,0:T(8,128)S(1)}, f32[1024,128]{1,0:T(8,128)}, u32[]{:S(2)}) copy-start(f32[1024,128]{1,0:T(8,128)} %nodes.5) | copy-start | bytes 1572868
  21.7 6.8 %copy-start.17 = (f32[128,128]{1,0:T(8,128)S(1)}, f32[128,128]{1,0:T(8,128)}, u32[]{:S(2)}) copy-start(f32[128,128]{1,0:T(8,128)} %node_out.2) | copy-start | bytes 196612
  21.7 6.8 %copy-start.18 = (s32[6,1024]{1,0:T(8,128)S(1)}, s32[6,1024]{1,0:T(8,128)}, u32[]{:S(2)}) copy-start(s32[6,1024]{1,0:T(8,128)} %nbr.1) | copy-start | bytes 73732
  24.9 1.6 %copy-start.21 = (f32[6,1024,128]{2,1,0:T(8,128)}, f32[6,1024,128]{2,1,0:T(8,128)S(1)}, u32[]{:S(2)}) copy-start(f32[6,1024,128]{2,1,0:T(8,128)S(1)} %get-tuple-element.25.pre) | copy-start | bytes 9437188
  28.5 1.9 %copy-start.12 = (f32[6,1024,128]{2,1,0:T(8,128)S(1)}, f32[6,1024,128]{2,1,0:T(8,128)}, u32[]{:S(2)}) copy-start(f32[6,1024,128]{2,1,0:T(8,128)} %edges.3) | copy-start | bytes 9437188
  30.3 1.9 %copy-start.22 = (f32[6,1024,128]{2,1,0:T(8,128)S(1)}, f32[6,1024,128]{2,1,0:T(8,128)}, u32[]{:S(2)}) copy-start(f32[6,1024,128]{2,1,0:T(8,128)} %copy-done.21) | copy-start | bytes 9437188
  32.2 35.6 %copy-start.3 = (f32[256,128]{1,0:T(8,128)S(1)}, f32[256,128]{1,0:T(8,128)}, u32[]{:S(2)}) copy-start(f32[256,128]{1,0:T(8,128)} %edge_in.5) | copy-start | bytes 393220
  32.2 35.6 %copy-start.4 = (f32[256,128]{1,0:T(8,128)S(1)}, f32[256,128]{1,0:T(8,128)}, u32[]{:S(2)}) copy-start(f32[256,128]{1,0:T(8,128)} %node_in.3) | copy-start | bytes 393220
  32.2 35.6 %copy-start.5 = (f32[128,128]{1,0:T(8,128)S(1)}, f32[128,128]{1,0:T(8,128)}, u32[]{:S(2)}) copy-start(f32[128,128]{1,0:T(8,128)} %edge_out.3) | copy-start | bytes 196612
  32.2 35.6 %copy-start.6 = (f32[128,128]{1,0:T(8,128)S(1)}, f32[128,128]{1,0:T(8,128)}, u32[]{:S(2)}) copy-start(f32[128,128]{1,0:T(8,128)} %node_out.3) | copy-start | bytes 196612
  50.0 8.9 %collective-permute-start.1 = (f32[128,128]{1,0:T(8,128)S(1)}, f32[128,128]{1,0:T(8,128)S(1)}, u32[]{:S(2)}, u32[]{:S(2)}) collective-permute-start(f32[128,128]{1,0:T(8,128)S(1)} %get-tuple-element.36), channel_id=1, source_target_pairs={{4,8},{8,4},{12,16},{16,12},{20,24},{24,20},{28,32},{32,28},{36,40... | collective-permute-start | bytes 196616 | tf_op jit(solution)/shard_map/ppermute | solution.py:358
  59.3 8.6 %collective-permute-start.2 = (f32[64,128]{1,0:T(8,128)S(1)}, f32[64,128]{1,0:T(8,128)S(1)}, u32[]{:S(2)}, u32[]{:S(2)}) collective-permute-start(f32[64,128]{1,0:T(8,128)S(1)} %get-tuple-element.39), channel_id=1, source_target_pairs={{4,8},{8,4},{12,16},{16,12},{20,24},{24,20},{28,32},{32,28},{36,40... | collective-permute-start | bytes 98312 | tf_op jit(solution)/shard_map/ppermute | solution.py:358
  69.9 8.9 %collective-permute-start.3 = (f32[128,128]{1,0:T(8,128)S(1)}, f32[128,128]{1,0:T(8,128)S(1)}, u32[]{:S(2)}, u32[]{:S(2)}) collective-permute-start(f32[128,128]{1,0:T(8,128)S(1)} %get-tuple-element.42), channel_id=1, source_target_pairs={{4,8},{8,4},{12,16},{16,12},{20,24},{24,20},{28,32},{32,28},{36,40... | collective-permute-start | bytes 196616 | tf_op jit(solution)/shard_map/ppermute | solution.py:358
